TPU v7x, 256 devices: a whole 4x4x8 slice. The times are simulated.
256 devices in a mesh: sub: 32 (over y, x, core), grp: 8 (over z).
Axes of the slice: x: 4, y: 4, z: 8, core: 2. Of those that a mesh axis runs over, the one named last changes fastest.
Arguments:
- residual: bfloat16 [8, 32, 1024, 512], P('grp', 'sub'), may hold values from -6 to 6
- face_order: int32 [8, 32, 1024], P('grp', 'sub'), may hold values from 0 to 1023, each once within a row
- stiffness: float32 [8, 32], replicated, may hold values from 1 to 100
- schur: bfloat16 [8, 32, 1024, 1024], P('grp', 'sub')
- local_inverse: bfloat16 [8, 32, 1024, 1024], P('grp', 'sub')
- coarse_basis: bfloat16 [8, 32, 1024, 128], P('grp', 'sub'), may hold values from -0.1875 to 0.1875
- coarse_map: int32 [8, 32, 128], P('grp', 'sub'), may hold values from 0 to 511, as said below
- level2_inverse: float32 [8, 512, 512], P('grp')
- level2_basis: float32 [8, 512, 128], P('grp'), may hold values from -0.25 to 0.25
- level2_map: int32 [8, 128], P('grp'), may hold values from 0 to 511, as said below
- level3_inverse: float32 [512, 512], replicated
Outputs:
- solution: bfloat16 [8, 32, 1024, 512], P('grp', 'sub')
- image: bfloat16 [8, 32, 1024, 512], P('grp', 'sub')
Inputs may be any that keep to these rules, and one draw needn't show every extreme that they name: `face_order`: each subdomain's row holds every number of 0 to 1023 once. `coarse_map`: within one subdomain the 128 entries are distinct, and each of a group's 512 level-2 coarse values is named by some subdomain of the group. `level2_map`: within one group the 128 entries are distinct, and each level-3 coarse value is named by some group.
All inputs are finite; a program needn't handle non-finite values.
Results may differ from a plain program's by a relative error of at most 0.0062.
Values may be sent and summed in bfloat16 or wider, within the bound.
A program may use at most 64 MiB of HBM per device.

v0:
```python
import jax
import jax.numpy as jnp
from jax import lax
from jax.sharding import PartitionSpec as P

highest = lax.Precision.HIGHEST


def extended(cells, sides, width):
    for axis, dim in sides:
        count = lax.axis_size(axis)
        ends = count - 1
        head = lax.slice_in_dim(cells, 0, width, axis=dim)
        tail = lax.slice_in_dim(cells, cells.shape[dim] - width, cells.shape[dim], axis=dim)
        cells = jnp.concatenate(
            [
                lax.ppermute(tail, axis, [(i, (i + 1) % count) for i in range(ends)]),
                cells,
                lax.ppermute(head, axis, [((i + 1) % count, i) for i in range(ends)]),
            ],
            axis=dim,
        )
    return cells


def face_weights(stiffness, group_index, member_index):
    group_count, member_count = stiffness.shape
    itself = stiffness[group_index, member_index]

    def share_of(other_group, other_member, present):
        neighbour = stiffness[
            jnp.clip(other_group, 0, group_count - 1), jnp.clip(other_member, 0, member_count - 1)
        ]
        return jnp.where(present, itself / (itself + neighbour), jnp.float32(1.0))

    return jnp.stack(
        [
            share_of(group_index, member_index - 1, member_index > 0),
            share_of(group_index, member_index + 1, member_index < member_count - 1),
            share_of(group_index - 1, member_index, group_index > 0),
            share_of(group_index + 1, member_index, group_index < group_count - 1),
        ]
    )


def shards(
    residual,
    face_order,
    stiffness,
    schur,
    local_inverse,
    coarse_basis,
    coarse_map,
    level2_inverse,
    level2_basis,
    level2_map,
    level3_inverse,
):
    resid_block = residual[0, 0]
    interface_size, columns = resid_block.shape
    face_size = interface_size // 4
    ordering = face_order[0, 0]
    inverse = jnp.argsort(ordering)
    group_index = lax.axis_index("grp")
    member_index = lax.axis_index("sub")
    weights = face_weights(stiffness, group_index, member_index)
    face_of = inverse // face_size
    dof_weight = jnp.sum(
        jnp.where(face_of[:, None] == jnp.arange(4)[None, :], weights[None, :], jnp.float32(0.0)),
        axis=1,
    )
    weighted = (dof_weight[:, None] * resid_block.astype(jnp.float32)).astype(jnp.bfloat16)
    contract_rows = (((0,), (0,)), ((), ()))
    coarse_base = coarse_basis[0, 0]
    coarse_res = lax.dot_general(
        coarse_base, weighted, contract_rows, preferred_element_type=jnp.float32
    )
    level2_size = level2_inverse.shape[1]
    local_map = coarse_map[0, 0]
    selector = (local_map[None, :] == jnp.arange(level2_size)[:, None]).astype(jnp.float32)
    contribution = jnp.dot(selector, coarse_res, precision=highest)
    group_base = level2_basis[0]
    group_map = level2_map[0]
    level3_size = level3_inverse.shape[0]
    selector_three = (group_map[None, :] == jnp.arange(level3_size)[:, None]).astype(jnp.float32)
    local_part = jnp.dot(local_inverse[0, 0], weighted, preferred_element_type=jnp.float32)
    group_inverse = level2_inverse[0]
    level2_res = lax.psum(contribution, "sub")
    group_terms = lax.dot_general(group_base, level2_res, contract_rows, precision=highest)
    level3_res = lax.psum(jnp.dot(selector_three, group_terms, precision=highest), "grp")
    level2_local = jnp.dot(group_inverse, level2_res, precision=highest)
    level3_sol = jnp.dot(level3_inverse, level3_res, precision=highest)
    level2_sol = level2_local + jnp.dot(group_base, level3_sol[group_map], precision=highest)
    coarse_part = jnp.dot(coarse_base.astype(jnp.float32), level2_sol[local_map], precision=highest)
    sendable = (dof_weight[:, None] * (local_part + coarse_part)).astype(jnp.bfloat16)
    face_blocks = sendable[ordering].reshape(4, face_size, columns)
    sub_padded = extended(face_blocks[0:2], (("sub", 0),), 1)
    grp_padded = extended(face_blocks[2:4], (("grp", 0),), 1)
    received = jnp.stack([sub_padded[0], sub_padded[3], grp_padded[0], grp_padded[3]])
    summed = (face_blocks.astype(jnp.float32) + received.astype(jnp.float32)).astype(jnp.bfloat16)
    solution = summed.reshape(interface_size, columns)[inverse]
    image = jnp.dot(schur[0, 0], solution, preferred_element_type=jnp.float32).astype(jnp.bfloat16)
    return (solution[None, None], image[None, None])


def solution(mesh):
    placed = (
        P("grp", "sub", None, None),
        P("grp", "sub", None),
        P(),
        P("grp", "sub", None, None),
        P("grp", "sub", None, None),
        P("grp", "sub", None, None),
        P("grp", "sub", None),
        P("grp", None, None),
        P("grp", None, None),
        P("grp", None),
        P(),
    )
    return jax.shard_map(
        shards,
        mesh=mesh,
        in_specs=placed,
        out_specs=(P("grp", "sub", None, None), P("grp", "sub", None, None)),
        check_vma=False,
    )
```

profile of v0, /device:TPU:8, one launch (start us, length us, event | category | flops | bytes accessed | tf_op | source)
XLA Modules:
  0.0 290.3 jit_solution(15084661443975097650)
XLA Ops:
  7.2 0.0 copy-start
  7.2 0.0 all-reduce.3.cloned.1.call-start
  7.2 1.6 fusion.33
  16.3 5.1 %sort.17 = (s32[1024]{0:T(1024)}, s32[1024]{0:T(1024)S(1)}) sort(s32[1024]{0:T(1024)} %bitcast.82, s32[1024]{0:T(1024)S(1)} %iota.13), dimensions={0}, to_apply=%region_0.0 | sort | flops 10240 | bytes 16384 | tf_op jit(solution)/shard_map/jit(argsort)/sort | solution.py:63
  21.4 0.0 copy-start.6
  21.4 0.1 pad_maximum_fusion.1
  21.5 0.0 copy-start.4
  21.5 0.1 select_reduce_fusion
  21.6 1.9 fusion.15
  23.6 2.2 fusion.24
  25.8 0.0 all-reduce.3.cloned.1.call-update
  25.8 0.0 copy-start.7
  25.8 0.0 copy-start.5
  25.8 0.0 all-reduce.5.cloned.1.call-start
  25.9 0.0 copy-done.6
  25.9 117.2 %all-reduce.3.cloned.1.call-done = f32[512,512]{1,0:T(8,128)} async-done(((f32[512,512]{1,0:T(8,128)}), f32[512,512]{1,0:T(8,128)}) %all-reduce.3.cloned.1.call-update) | async-done | bytes 1048592 | tf_op jit(solution)/shard_map/psum | solution.py:88
  143.2 0.0 copy-done.4
  143.2 3.0 %fusion.20 = f32[512,128]{1,0:T(8,128)S(1)} fusion(f32[512,512]{1,0:T(8,128)} %all-reduce.3.cloned.1.call-done, f32[1,512,128]{2,1,0:T(8,128)S(1)} %copy-done.4), kind=kOutput, calls=%fused_computation.28 | convolution fusion | flops 402653184 | bytes 1572864 | tf_op jit(solution)/shard_map/dot_general | solution.py:89
  146.2 1.6 fusion.25
  147.8 0.0 all-reduce.5.cloned.1.call-update
  147.8 0.0 copy-done.7
  147.8 0.0 copy-done.5
  147.9 0.0 copy-done
  147.9 0.0 copy-start.3
  147.9 4.2 %fusion.3 = f32[512,1024]{1,0:T(8,128)} fusion(bf16[1,1,1024,1024]{3,2,1,0:T(8,128)(2,1)S(1)} %copy-done, bf16[1,1,1024,512]{3,2,1,0:T(8,128)(2,1)} %param.11, f32[1024]{0:T(1024)S(1)} %select_reduce_fusion), kind=kOutput, calls=%fused_computation.8 | convolution fusion | flops 1075314688 | bytes 5246976 | tf_op jit(solution)/shard_map/dot_general | solution.py:86
  152.1 72.2 %all-reduce.5.cloned.1.call-done = f32[512,512]{1,0:T(8,128)} async-done(((f32[512,512]{1,0:T(8,128)}), f32[512,512]{1,0:T(8,128)}) %all-reduce.5.cloned.1.call-update) | async-done | bytes 1048592 | tf_op jit(solution)/shard_map/psum | solution.py:90
  224.3 0.0 copy-done.3
  224.3 5.7 %convolution_bitcast_fusion = f32[512,512]{0,1:T(8,128)} fusion(f32[512,512]{1,0:T(8,128)} %all-reduce.5.cloned.1.call-done, f32[512,512]{1,0:T(8,128)S(1)} %copy-done.3), kind=kOutput, calls=%fused_computation.15 | convolution fusion | flops 1610612736 | bytes 3145728 | tf_op jit(solution)/shard_map/dot_general | solution.py:92
  230.0 1.6 copy.17
  231.5 0.8 gather_fusion
  232.3 0.0 copy-start.2
  232.3 2.1 fusion.18
  234.4 0.0 copy-done.2
  234.4 5.7 %fusion.12 = f32[512,512]{0,1:T(8,128)} fusion(f32[512,512]{1,0:T(8,128)S(1)} %fusion.18, f32[512,512]{1,0:T(8,128)S(1)} %copy-done.2, f32[1,512,512]{2,1,0:T(8,128)} %param.18), kind=kOutput, calls=%fused_computation.17 | convolution fusion | flops 1610874880 | bytes 4194304 | tf_op jit(solution)/shard_map/dot_general | solution.py:91
  240.1 1.7 copy.18
  241.8 0.8 gather_fusion.1
  242.5 3.7 %fusion.11 = bf16[1024,512]{0,1:T(8,128)(2,1)} fusion(f32[512,1024]{1,0:T(8,128)} %fusion.3, f32[128,512]{1,0:T(8,128)S(1)} %gather_fusion.1, f32[1024]{0:T(1024)S(1)} %select_reduce_fusion, bf16[1,1,1024,128]{3,2,1,0:T(8,128)(2,1)} %param.16), kind=kOutput, calls=%fused_computation.14 | convolution fusion | flops 806879232 | bytes 3674112 | tf_op jit(solution)/shard_map/dot_general | solution.py:94
  246.3 1.5 copy.19
  247.8 5.1 %gather_fusion.2 = bf16[1024,512]{1,0:T(8,128)(2,1)} fusion(bf16[1024,512]{1,0:T(8,128)(2,1)S(1)} %copy.19, s32[1024]{0:T(1024)S(1)} %broadcast_clamp_fusion), kind=kCustom, calls=%fused_computation.2 | custom fusion | bytes 2101248 | tf_op jit(solution)/shard_map/gather | solution.py:96
  252.9 0.0 copy-start.1
  252.9 1.3 slice_bitcast_fusion.3
  254.2 1.9 collective-permute-start
  256.2 5.8 %collective-permute-start.1 = (bf16[1,256,512]{2,1,0:T(8,128)(2,1)S(1)}, bf16[1,256,512]{2,1,0:T(8,128)(2,1)S(1)}, u32[]{:S(2)}, u32[]{:S(2)}) collective-permute-start(bf16[1,256,512]{2,1,0:T(8,128)(2,1)S(1)} %get-tuple-element.12), channel_id=1, source_target_pairs={{8,0},{16,8},{24,16},{32,24},{40,32},{48,40},{56,48},{64,56},{72,6... | collective-permute-start | bytes 786440 | tf_op jit(solution)/shard_map/ppermute | solution.py:19
  261.9 3.1 %collective-permute-start.2 = (bf16[1,256,512]{2,1,0:T(8,128)(2,1)S(1)}, bf16[1,256,512]{2,1,0:T(8,128)(2,1)S(1)}, u32[]{:S(2)}, u32[]{:S(2)}) collective-permute-start(bf16[1,256,512]{2,1,0:T(8,128)(2,1)S(1)} %get-tuple-element.11), channel_id=1, source_target_pairs={{0,1},{1,2},{2,3},{3,4},{4,5},{5,6},{6,7},{8,9},{9,10},{10,11},{11... | collective-permute-start | bytes 786440 | tf_op jit(solution)/shard_map/ppermute | solution.py:17
  265.1 1.3 collective-permute-start.3
  266.4 0.0 collective-permute-done
  266.4 0.0 collective-permute-done.1
  266.4 2.5 collective-permute-done.2
  268.9 4.4 %collective-permute-done.3 = bf16[1,256,512]{2,1,0:T(8,128)(2,1)S(1)} collective-permute-done((bf16[1,256,512]{2,1,0:T(8,128)(2,1)S(1)}, bf16[1,256,512]{2,1,0:T(8,128)(2,1)S(1)}, u32[]{:S(2)}, u32[]{:S(2)}) %collective-permute-start.3) | collective-permute-done | bytes 262176 | tf_op jit(solution)/shard_map/ppermute | solution.py:19
  273.3 0.1 pad_maximum_fusion
  273.5 0.0 copy-done.1
  273.5 0.4 fusion
  273.9 5.1 %gather_fusion.3 = bf16[1024,512]{1,0:T(8,128)(2,1)} fusion(bf16[1024,512]{1,0:T(8,128)(2,1)S(1)} %fusion, s32[1024]{0:T(1024)S(1)} %get-tuple-element.14), kind=kCustom, calls=%fused_computation.3 | custom fusion | bytes 2101248 | tf_op jit(solution)/shard_map/gather | solution.py:101
  278.9 3.2 %fusion.8 = bf16[1,1,1024,512]{2,3,1,0:T(8,128)(2,1)S(1)} fusion(bf16[1024,512]{1,0:T(8,128)(2,1)} %gather_fusion.3, bf16[1,1,1024,1024]{3,2,1,0:T(8,128)(2,1)} %param.14), kind=kOutput, calls=%fused_computation.13 | convolution fusion | flops 1074266112 | bytes 4194304 | tf_op jit(solution)/shard_map/dot_general | solution.py:102
  282.2 1.3 copy.20
  (8 shorter events, 0.0 us)
Async XLA Ops:
  7.2 140.7 %copy-start = (bf16[1,1,1024,1024]{3,2,1,0:T(8,128)(2,1)S(1)}, bf16[1,1,1024,1024]{3,2,1,0:T(8,128)(2,1)}, u32[]{:S(2)}) copy-start(bf16[1,1,1024,1024]{3,2,1,0:T(8,128)(2,1)} %param.15) | copy-start | bytes 6291460
  7.2 136.0 %all-reduce.3.cloned.1.call-start = ((), (), s32[]{:S(2)}) async-start(), calls=%async_computation | async-start | bytes 2097152 | tf_op jit(solution)/shard_map/psum | solution.py:88
  21.4 4.5 %copy-start.6 = (s32[1,128]{1,0:T(1,128)S(1)}, s32[1,128]{1,0:T(1,128)}, u32[]{:S(2)}) copy-start(s32[1,128]{1,0:T(1,128)} %param.20) | copy-start | bytes 1540
  21.5 121.6 %copy-start.4 = (f32[1,512,128]{2,1,0:T(8,128)S(1)}, f32[1,512,128]{2,1,0:T(8,128)}, u32[]{:S(2)}) copy-start(f32[1,512,128]{2,1,0:T(8,128)} %param.19) | copy-start | bytes 786436
  25.8 122.0 %copy-start.7 = (s32[1,1,128]{2,1,0:T(1,128)S(1)}, s32[1,1,128]{2,1,0:T(1,128)}, u32[]{:S(2)}) copy-start(s32[1,1,128]{2,1,0:T(1,128)} %param.17) | copy-start | bytes 1540
  25.8 122.0 %copy-start.5 = (s32[1,1,1024]{2,1,0:T(1,128)S(1)}, s32[1,1,1024]{2,1,0:T(1,128)}, u32[]{:S(2)}) copy-start(s32[1,1,1024]{2,1,0:T(1,128)} %param.12) | copy-start | bytes 12292
  25.8 198.5 %all-reduce.5.cloned.1.call-start = ((), (), s32[]{:S(2)}) async-start(), calls=%async_computation.1 | async-start | bytes 2097152 | tf_op jit(solution)/shard_map/psum | solution.py:90
  147.9 76.4 %copy-start.3 = (f32[512,512]{1,0:T(8,128)S(1)}, f32[512,512]{1,0:T(8,128)}, u32[]{:S(2)}) copy-start(f32[512,512]{1,0:T(8,128)} %param.21) | copy-start | bytes 3145732
  232.3 2.1 copy-start.2
  252.9 20.6 %copy-start.1 = (bf16[1024,512]{1,0:T(8,128)(2,1)S(1)}, bf16[1024,512]{1,0:T(8,128)(2,1)}, u32[]{:S(2)}) copy-start(bf16[1024,512]{1,0:T(8,128)(2,1)} %gather_fusion.2) | copy-start | bytes 3145732
  254.2 12.1 %collective-permute-start = (bf16[1,256,512]{2,1,0:T(8,128)(2,1)S(1)}, bf16[1,256,512]{2,1,0:T(8,128)(2,1)S(1)}, u32[]{:S(2)}, u32[]{:S(2)}) collective-permute-start(bf16[1,256,512]{2,1,0:T(8,128)(2,1)S(1)} %get-tuple-element.10), channel_id=1, source_target_pairs={{0,8},{8,16},{16,24},{24,32},{32,40},{40,48},{48,56},{56,64},{64,7... | collective-permute-start | bytes 786440 | tf_op jit(solution)/shard_map/ppermute | solution.py:17
  256.2 10.2 %collective-permute-start.1 = (bf16[1,256,512]{2,1,0:T(8,128)(2,1)S(1)}, bf16[1,256,512]{2,1,0:T(8,128)(2,1)S(1)}, u32[]{:S(2)}, u32[]{:S(2)}) collective-permute-start(bf16[1,256,512]{2,1,0:T(8,128)(2,1)S(1)} %get-tuple-element.12), channel_id=1, source_target_pairs={{8,0},{16,8},{24,16},{32,24},{40,32},{48,40},{56,48},{64,56},{72,6... | collective-permute-start | bytes 786440 | tf_op jit(solution)/shard_map/ppermute | solution.py:19
  261.9 7.0 %collective-permute-start.2 = (bf16[1,256,512]{2,1,0:T(8,128)(2,1)S(1)}, bf16[1,256,512]{2,1,0:T(8,128)(2,1)S(1)}, u32[]{:S(2)}, u32[]{:S(2)}) collective-permute-start(bf16[1,256,512]{2,1,0:T(8,128)(2,1)S(1)} %get-tuple-element.11), channel_id=1, source_target_pairs={{0,1},{1,2},{2,3},{3,4},{4,5},{5,6},{6,7},{8,9},{9,10},{10,11},{11... | collective-permute-start | bytes 786440 | tf_op jit(solution)/shard_map/ppermute | solution.py:17
  265.1 8.3 %collective-permute-start.3 = (bf16[1,256,512]{2,1,0:T(8,128)(2,1)S(1)}, bf16[1,256,512]{2,1,0:T(8,128)(2,1)S(1)}, u32[]{:S(2)}, u32[]{:S(2)}) collective-permute-start(bf16[1,256,512]{2,1,0:T(8,128)(2,1)S(1)} %get-tuple-element.13), channel_id=1, source_target_pairs={{1,0},{2,1},{3,2},{4,3},{5,4},{6,5},{7,6},{9,8},{10,9},{11,10},{12... | collective-permute-start | bytes 786440 | tf_op jit(solution)/shard_map/ppermute | solution.py:19
Sparse Core Ops, SparseCore 0:
  25.9 117.1 all-reduce.2
  147.9 76.3 all-reduce.4
where the time goes:
time: 291 us; the launch traced here: 290 us
  waiting for transfers between devices  196 us (67%)
  matrix products  33.3 us (11%)
  between operations  21.9 us (8%)
  local copies, waits for them, and re-layouts  20.7 us (7%)
  starting transfers between devices  12.2 us (4%)
  other arithmetic  5.76 us (2%)
    psum x1, waiting for transfers between devices, shards(): level2_res = lax.psum(contribution, 'sub')  117 us
    psum x1, waiting for transfers between devices, shards(): lax.psum(jnp.dot(selector_three, group_terms, precision=highest), 'grp')  72.2 us
    ppermute x2, starting transfers between devices, extended(): lax.ppermute(head, axis, [((i + 1) % count, i) for i in range(ends)])  7.04 us
  transfers between devices with their start and end apart: 6, of which 4 were waited for; matrix products, arithmetic and copies ran while one was open for 1% of the time, Pallas kernels for 0%

commit v1 on v0

--- a/solution.py
+++ b/solution.py
@@ -87,7 +87,9 @@
     group_inverse = level2_inverse[0]
     level2_res = lax.psum(contribution, "sub")
     group_terms = lax.dot_general(group_base, level2_res, contract_rows, precision=highest)
-    level3_res = lax.psum(jnp.dot(selector_three, group_terms, precision=highest), "grp")
+    level3_res = jnp.sum(
+        lax.all_gather(jnp.dot(selector_three, group_terms, precision=highest), "grp"), axis=0
+    )
     level2_local = jnp.dot(group_inverse, level2_res, precision=highest)
     level3_sol = jnp.dot(level3_inverse, level3_res, precision=highest)
     level2_sol = level2_local + jnp.dot(group_base, level3_sol[group_map], precision=highest)

time: 291 us -> 313 us (1.076)
  waiting for transfers between devices: 196 us -> 215 us
  other arithmetic: 5.76 us -> 10.3 us
    all_gather x0 -> x1, waiting for transfers between devices: none -> 90.5 us  [shards(): lax.all_gather(jnp.dot(selector_three, group_terms, precision=highest), '...]
    psum x1 -> x0, waiting for transfers between devices: 72.2 us -> none  [shards(): lax.psum(jnp.dot(selector_three, group_terms, precision=highest), 'grp')]
    reduce_sum x0 -> x1, other arithmetic: none -> 4.49 us  [shards(): jnp.sum(lax.all_gather(jnp.dot(selector_three, group_terms, precision=hig...]
  transfers between devices with their start and end apart: 6 -> 6, of which waited for: 4 -> 5; matrix products, arithmetic and copies ran while one was open for 1% -> 1% of each run, Pallas kernels for 0% -> 0%
where the time goes in v1:
time: 313 us; the launch traced here: 311 us
  waiting for transfers between devices  215 us (69%)
  matrix products  33.4 us (11%)
  between operations  21.7 us (7%)
  local copies, waits for them, and re-layouts  20.5 us (7%)
  starting transfers between devices  10.7 us (3%)
  other arithmetic  10.3 us (3%)
    psum x1, waiting for transfers between devices, shards(): level2_res = lax.psum(contribution, 'sub')  117 us
    all_gather x1, waiting for transfers between devices, shards(): lax.all_gather(jnp.dot(selector_three, group_terms, precision=highest), '...  90.5 us
    ppermute x2, starting transfers between devices, extended(): lax.ppermute(head, axis, [((i + 1) % count, i) for i in range(ends)])  7.04 us
  transfers between devices with their start and end apart: 6, of which 5 were waited for; matrix products, arithmetic and copies ran while one was open for 1% of the time, Pallas kernels for 0%

profile of v1, /device:TPU:8, one launch (start us, length us, event | category | flops | bytes accessed | tf_op | source)
XLA Modules:
  0.0 311.4 jit_solution(3058454516985966188)
XLA Ops:
  7.2 0.0 copy-start
  7.2 0.0 all-reduce.2.cloned.1.call-start
  7.2 1.5 fusion.33
  16.1 5.1 %sort.17 = (s32[1024]{0:T(1024)}, s32[1024]{0:T(1024)S(1)}) sort(s32[1024]{0:T(1024)} %bitcast.84, s32[1024]{0:T(1024)S(1)} %iota.13), dimensions={0}, to_apply=%region_0.0 | sort | flops 10240 | bytes 16384 | tf_op jit(solution)/shard_map/jit(argsort)/sort | solution.py:63
  21.2 0.0 copy-start.3
  21.2 0.1 pad_maximum_fusion.1
  21.3 0.1 select_reduce_fusion
  21.4 1.9 fusion.15
  23.4 0.0 copy-start.5
  23.4 2.2 fusion.24
  25.6 0.0 all-reduce.2.cloned.1.call-update
  25.6 0.0 copy-start.6
  25.6 0.0 copy-start.4
  25.6 0.0 all-gather.3.cloned.1.call-start
  25.7 117.2 %all-reduce.2.cloned.1.call-done = f32[512,512]{1,0:T(8,128)} async-done(((f32[512,512]{1,0:T(8,128)}), f32[512,512]{1,0:T(8,128)}) %all-reduce.2.cloned.1.call-update) | async-done | bytes 1048592 | tf_op jit(solution)/shard_map/psum | solution.py:88
  142.9 0.0 copy-done.3
  142.9 3.0 fusion.20
  145.9 0.0 copy-done.5
  145.9 1.6 fusion.25
  147.5 0.0 all-gather.3.cloned.1.call-update
  147.6 0.0 copy-done.6
  147.6 0.0 copy-done.4
  147.6 0.0 copy-done
  147.7 4.1 %fusion.3 = f32[512,1024]{1,0:T(8,128)} fusion(bf16[1,1,1024,1024]{3,2,1,0:T(8,128)(2,1)S(1)} %copy-done, bf16[1,1,1024,512]{3,2,1,0:T(8,128)(2,1)} %param.11, f32[1024]{0:T(1024)S(1)} %select_reduce_fusion), kind=kOutput, calls=%fused_computation.8 | convolution fusion | flops 1075314688 | bytes 5246976 | tf_op jit(solution)/shard_map/dot_general | solution.py:86
  151.8 90.5 %all-gather.3.cloned.1.call-done = f32[4096,512]{1,0:T(8,128)} async-done(((f32[512,512]{1,0:T(8,128)}), f32[4096,512]{1,0:T(8,128)}) %all-gather.3.cloned.1.call-update) | async-done | bytes 8388624 | tf_op jit(solution)/shard_map/all_gather | solution.py:91
  242.3 4.5 %reduce_sum.19 = f32[512,512]{1,0:T(8,128)S(1)} reduce(f32[8,512,512]{2,1,0:T(8,128)} %bitcast.82, f32[]{:T(128)} %constant.49.clone.1), dimensions={0}, to_apply=%region_3.4 | reduce | flops 1835008 | bytes 9437188 | tf_op jit(solution)/shard_map/reduce_sum | solution.py:90
  246.8 5.7 %convolution_bitcast_fusion = f32[512,512]{0,1:T(8,128)} fusion(f32[512,512]{1,0:T(8,128)S(1)} %reduce_sum.19, f32[512,512]{1,0:T(8,128)} %param.21), kind=kOutput, calls=%fused_computation.15 | convolution fusion | flops 1610612736 | bytes 3145728 | tf_op jit(solution)/shard_map/dot_general | solution.py:94
  252.5 1.6 copy.17
  254.0 0.8 gather_fusion
  254.8 0.0 copy-start.2
  254.8 2.1 fusion.18
  256.9 0.0 copy-done.2
  256.9 5.9 %fusion.12 = f32[512,512]{0,1:T(8,128)} fusion(f32[512,512]{1,0:T(8,128)S(1)} %fusion.18, f32[512,512]{1,0:T(8,128)S(1)} %copy-done.2, f32[1,512,512]{2,1,0:T(8,128)} %param.18), kind=kOutput, calls=%fused_computation.17 | convolution fusion | flops 1610874880 | bytes 4194304 | tf_op jit(solution)/shard_map/dot_general | solution.py:93
  262.7 1.6 copy.18
  264.3 0.8 gather_fusion.1
  265.1 3.7 %fusion.11 = bf16[1024,512]{0,1:T(8,128)(2,1)} fusion(f32[512,1024]{1,0:T(8,128)} %fusion.3, f32[128,512]{1,0:T(8,128)S(1)} %gather_fusion.1, f32[1024]{0:T(1024)S(1)} %select_reduce_fusion, bf16[1,1,1024,128]{3,2,1,0:T(8,128)(2,1)} %param.16), kind=kOutput, calls=%fused_computation.14 | convolution fusion | flops 806879232 | bytes 3674112 | tf_op jit(solution)/shard_map/dot_general | solution.py:96
  268.8 1.5 copy.19
  270.3 5.1 %gather_fusion.2 = bf16[1024,512]{1,0:T(8,128)(2,1)} fusion(bf16[1024,512]{1,0:T(8,128)(2,1)S(1)} %copy.19, s32[1024]{0:T(1024)S(1)} %broadcast_clamp_fusion), kind=kCustom, calls=%fused_computation.2 | custom fusion | bytes 2101248 | tf_op jit(solution)/shard_map/gather | solution.py:98
  275.4 0.0 copy-start.1
  275.4 1.3 slice_bitcast_fusion.3
  276.7 1.9 collective-permute-start
  278.7 5.8 %collective-permute-start.1 = (bf16[1,256,512]{2,1,0:T(8,128)(2,1)S(1)}, bf16[1,256,512]{2,1,0:T(8,128)(2,1)S(1)}, u32[]{:S(2)}, u32[]{:S(2)}) collective-permute-start(bf16[1,256,512]{2,1,0:T(8,128)(2,1)S(1)} %get-tuple-element.12), channel_id=1, source_target_pairs={{8,0},{16,8},{24,16},{32,24},{40,32},{48,40},{56,48},{64,56},{72,6... | collective-permute-start | bytes 786440 | tf_op jit(solution)/shard_map/ppermute | solution.py:19
  284.4 1.7 collective-permute-start.2
  286.1 1.3 collective-permute-start.3
  287.4 0.0 collective-permute-done
  287.4 0.9 collective-permute-done.1
  288.3 1.7 collective-permute-done.2
  290.0 4.4 %collective-permute-done.3 = bf16[1,256,512]{2,1,0:T(8,128)(2,1)S(1)} collective-permute-done((bf16[1,256,512]{2,1,0:T(8,128)(2,1)S(1)}, bf16[1,256,512]{2,1,0:T(8,128)(2,1)S(1)}, u32[]{:S(2)}, u32[]{:S(2)}) %collective-permute-start.3) | collective-permute-done | bytes 262176 | tf_op jit(solution)/shard_map/ppermute | solution.py:19
  294.4 0.1 pad_maximum_fusion
  294.5 0.0 copy-done.1
  294.5 0.4 fusion
  294.9 5.1 %gather_fusion.3 = bf16[1024,512]{1,0:T(8,128)(2,1)} fusion(bf16[1024,512]{1,0:T(8,128)(2,1)S(1)} %fusion, s32[1024]{0:T(1024)S(1)} %get-tuple-element.14), kind=kCustom, calls=%fused_computation.3 | custom fusion | bytes 2101248 | tf_op jit(solution)/shard_map/gather | solution.py:103
  300.0 3.2 %fusion.8 = bf16[1,1,1024,512]{2,3,1,0:T(8,128)(2,1)S(1)} fusion(bf16[1024,512]{1,0:T(8,128)(2,1)} %gather_fusion.3, bf16[1,1,1024,1024]{3,2,1,0:T(8,128)(2,1)} %param.14), kind=kOutput, calls=%fused_computation.13 | convolution fusion | flops 1074266112 | bytes 4194304 | tf_op jit(solution)/shard_map/dot_general | solution.py:104
  303.2 1.3 copy.20
  (8 shorter events, 0.0 us)
Async XLA Ops:
  7.2 140.5 %copy-start = (bf16[1,1,1024,1024]{3,2,1,0:T(8,128)(2,1)S(1)}, bf16[1,1,1024,1024]{3,2,1,0:T(8,128)(2,1)}, u32[]{:S(2)}) copy-start(bf16[1,1,1024,1024]{3,2,1,0:T(8,128)(2,1)} %param.15) | copy-start | bytes 6291460
  7.2 135.7 %all-reduce.2.cloned.1.call-start = ((), (), s32[]{:S(2)}) async-start(), calls=%async_computation | async-start | bytes 2097152 | tf_op jit(solution)/shard_map/psum | solution.py:88
  21.2 121.7 %copy-start.3 = (f32[1,512,128]{2,1,0:T(8,128)S(1)}, f32[1,512,128]{2,1,0:T(8,128)}, u32[]{:S(2)}) copy-start(f32[1,512,128]{2,1,0:T(8,128)} %param.19) | copy-start | bytes 786436
  23.4 122.6 %copy-start.5 = (s32[1,128]{1,0:T(1,128)S(1)}, s32[1,128]{1,0:T(1,128)}, u32[]{:S(2)}) copy-start(s32[1,128]{1,0:T(1,128)} %param.20) | copy-start | bytes 1540
  25.6 122.0 %copy-start.6 = (s32[1,1,128]{2,1,0:T(1,128)S(1)}, s32[1,1,128]{2,1,0:T(1,128)}, u32[]{:S(2)}) copy-start(s32[1,1,128]{2,1,0:T(1,128)} %param.17) | copy-start | bytes 1540
  25.6 122.0 %copy-start.4 = (s32[1,1,1024]{2,1,0:T(1,128)S(1)}, s32[1,1,1024]{2,1,0:T(1,128)}, u32[]{:S(2)}) copy-start(s32[1,1,1024]{2,1,0:T(1,128)} %param.12) | copy-start | bytes 12292
  25.6 216.7 %all-gather.3.cloned.1.call-start = ((), (), s32[]{:S(2)}) async-start(), calls=%async_computation.1 | async-start | bytes 9437184 | tf_op jit(solution)/shard_map/all_gather | solution.py:91
  254.8 2.1 copy-start.2
  275.4 19.1 %copy-start.1 = (bf16[1024,512]{1,0:T(8,128)(2,1)S(1)}, bf16[1024,512]{1,0:T(8,128)(2,1)}, u32[]{:S(2)}) copy-start(bf16[1024,512]{1,0:T(8,128)(2,1)} %gather_fusion.2) | copy-start | bytes 3145732
  276.7 10.7 %collective-permute-start = (bf16[1,256,512]{2,1,0:T(8,128)(2,1)S(1)}, bf16[1,256,512]{2,1,0:T(8,128)(2,1)S(1)}, u32[]{:S(2)}, u32[]{:S(2)}) collective-permute-start(bf16[1,256,512]{2,1,0:T(8,128)(2,1)S(1)} %get-tuple-element.10), channel_id=1, source_target_pairs={{0,8},{8,16},{16,24},{24,32},{32,40},{40,48},{48,56},{56,64},{64,7... | collective-permute-start | bytes 786440 | tf_op jit(solution)/shard_map/ppermute | solution.py:17
  278.7 9.6 %collective-permute-start.1 = (bf16[1,256,512]{2,1,0:T(8,128)(2,1)S(1)}, bf16[1,256,512]{2,1,0:T(8,128)(2,1)S(1)}, u32[]{:S(2)}, u32[]{:S(2)}) collective-permute-start(bf16[1,256,512]{2,1,0:T(8,128)(2,1)S(1)} %get-tuple-element.12), channel_id=1, source_target_pairs={{8,0},{16,8},{24,16},{32,24},{40,32},{48,40},{56,48},{64,56},{72,6... | collective-permute-start | bytes 786440 | tf_op jit(solution)/shard_map/ppermute | solution.py:19
  284.4 5.5 %collective-permute-start.2 = (bf16[1,256,512]{2,1,0:T(8,128)(2,1)S(1)}, bf16[1,256,512]{2,1,0:T(8,128)(2,1)S(1)}, u32[]{:S(2)}, u32[]{:S(2)}) collective-permute-start(bf16[1,256,512]{2,1,0:T(8,128)(2,1)S(1)} %get-tuple-element.11), channel_id=1, source_target_pairs={{0,1},{1,2},{2,3},{3,4},{4,5},{5,6},{6,7},{8,9},{9,10},{10,11},{11... | collective-permute-start | bytes 786440 | tf_op jit(solution)/shard_map/ppermute | solution.py:17
  286.1 8.3 %collective-permute-start.3 = (bf16[1,256,512]{2,1,0:T(8,128)(2,1)S(1)}, bf16[1,256,512]{2,1,0:T(8,128)(2,1)S(1)}, u32[]{:S(2)}, u32[]{:S(2)}) collective-permute-start(bf16[1,256,512]{2,1,0:T(8,128)(2,1)S(1)} %get-tuple-element.13), channel_id=1, source_target_pairs={{1,0},{2,1},{3,2},{4,3},{5,4},{6,5},{7,6},{9,8},{10,9},{11,10},{12... | collective-permute-start | bytes 786440 | tf_op jit(solution)/shard_map/ppermute | solution.py:19
Sparse Core Ops, SparseCore 0:
  25.7 117.1 all-reduce.1
  147.7 94.5 all-gather.2
